TPU v7x, 32 devices: a whole 2x2x4 slice. The times are simulated.
32 devices in a mesh: sec: 8 (over y, x, core), tile: 4 (over z).
Axes of the slice: x: 2, y: 2, z: 4, core: 2. Of those that a mesh axis runs over, the one named last changes fastest.
Arguments:
- descriptors: bfloat16 [16, 192, 128, 128], P('sec', 'tile'), may hold values from -8 to 8
- partner_step: int32 [16], replicated, may hold values from 0 to 2, as said below
Outputs:
- flow: float32 [16, 2, 192, 128], P('sec', None, 'tile')
Inputs may be any that keep to these rules, and one draw needn't show every extreme that they name: Every section is sound or damaged. partner_step is 0 for a damaged section; for a sound section it is the distance to the next sound section, or 0 where no sound section lies within 2 ahead inside the stack.
All inputs are finite; a program needn't handle non-finite values.
Results may differ from a plain program's by a relative error of at most 0.0003.
Values may be sent and summed in bfloat16 or wider, within the bound.
A program may use at most 64 MiB of HBM per device.

v0:
```python
import functools
import math

import jax
import jax.numpy as jnp
from jax import lax
from jax.experimental import pallas as pl
from jax.experimental.pallas import tpu as pltpu
from jax.sharding import PartitionSpec as P

WIN = 4
POOL = 8
SIDE = 2 * WIN + 1
PRIOR = 0.25
LOG2E = math.log2(math.e)
BAND = 32
LOW = -1e30


def coarse_shift(fixed_ref, moving_ref, count):
    cols = fixed_ref.shape[1]
    lanes = 12 * BAND

    def step(y, total):
        window = moving_ref[pl.ds(y, 12)].reshape(lanes, fixed_ref.shape[2])
        return total + lax.dot_general(
            fixed_ref[y], window, (((1,), (1,)), ((), ())), preferred_element_type=jnp.float32
        )

    table = lax.fori_loop(0, count, step, jnp.zeros((cols, lanes), jnp.float32))
    row = lax.broadcasted_iota(jnp.int32, (cols, lanes), 0)
    for bit in (1, 2, 4, 8):
        table = jnp.where((row & bit) != 0, pltpu.roll(table, lanes - bit, 1), table)
    scores = jnp.sum(table, axis=0, keepdims=True) * (
        1.0 / math.sqrt(fixed_ref.shape[2] * count * cols)
    )
    lane = lax.broadcasted_iota(jnp.int32, (1, lanes), 1) + BAND // 2
    lane = jnp.where(lane >= lanes, lane - lanes, lane)
    dy = (lane // BAND) - WIN
    dx = (lane % BAND) - BAND // 2
    valid = (dy <= WIN) & (jnp.abs(dx) <= WIN)
    scores = jnp.where(valid, scores, LOW)
    weights = jnp.exp(scores - jnp.max(scores, axis=1, keepdims=True))
    total = jnp.sum(weights, axis=1, keepdims=True)
    return (
        jnp.sum(weights * dy.astype(jnp.float32), axis=1, keepdims=True) / total,
        jnp.sum(weights * dx.astype(jnp.float32), axis=1, keepdims=True) / total,
    )


def fill_prior(prior_ref, shift_row, shift_col):
    shape = (256, 128)
    at = lax.broadcasted_iota(jnp.int32, shape, 0)
    cell = lax.broadcasted_iota(jnp.int32, shape, 1)
    dy = (at // 16) - (cell // 16) - WIN
    dx = (at % 16) - (cell % 8) - WIN
    valid = (jnp.abs(dy) <= WIN) & (jnp.abs(dx) <= WIN)
    far = (dy.astype(jnp.float32) - shift_row) ** 2 + (dx.astype(jnp.float32) - shift_col) ** 2
    prior_ref[...] = jnp.where(valid, far * (-PRIOR * LOG2E), LOW)


def widen_row(wide_ref, at, row):
    row = row.astype(jnp.float32)
    edge = jnp.zeros((WIN, row.shape[1]), jnp.float32)
    left = jnp.concatenate([edge, row[:-WIN]], axis=0)
    right = jnp.concatenate([row[WIN:], edge], axis=0)
    wide_ref[at] = jnp.concatenate([left, right], axis=1).astype(jnp.bfloat16)


def tile_flow(window, fixed, prior_ref):
    cell = lax.broadcasted_iota(jnp.int32, fixed.shape, 0)
    first = ((cell % 16) < 8).astype(jnp.float32).astype(jnp.bfloat16)
    both = jnp.concatenate([fixed * first, fixed * (jnp.bfloat16(1.0) - first)], axis=1)
    corr = lax.dot_general(
        window, both, (((1,), (1,)), ((), ())), preferred_element_type=jnp.float32
    )
    scores = corr * (LOG2E / math.sqrt(fixed.shape[1])) + prior_ref[...]
    weights = jnp.exp2(scores - jnp.max(scores, axis=0, keepdims=True)).reshape(16, 16, 128)
    down = weights[15]
    rows = down
    for at in range(14, 0, -1):
        down = down + weights[at]
        rows = rows + down
    down = down + weights[0]
    inverse = 1.0 / jnp.sum(down, axis=0, keepdims=True)
    at = lax.broadcasted_iota(jnp.int32, (16, 128), 0).astype(jnp.float32)
    cell = lax.broadcasted_iota(jnp.int32, (1, 128), 1)
    flow_row = jnp.sum(rows, axis=0, keepdims=True) * inverse
    flow_col = jnp.sum(down * at, axis=0, keepdims=True) * inverse
    return (
        flow_row - ((cell // 16) + WIN).astype(jnp.float32),
        flow_col - ((cell % 8) + WIN).astype(jnp.float32),
    )


def pair_kernel(fixed_ref, low_ref, moving_ref, high_ref, fixed_all, moving_all, out_ref, wide, prior):
    rows = fixed_ref.shape[0]
    groups = fixed_ref.shape[1] // 16
    shift_row, shift_col = coarse_shift(fixed_all, moving_all, fixed_all.shape[0])
    fill_prior(prior, shift_row, shift_col)
    for r in range(WIN):
        widen_row(wide, r, low_ref[r])
        widen_row(wide, rows + WIN + r, high_ref[r])

    def widen(r, carry):
        widen_row(wide, r + WIN, moving_ref[r])
        return carry

    lax.fori_loop(0, rows, widen, 0)

    def group(g, carry):
        top = pl.multiple_of(g * 8, 8)
        flow_rows, flow_cols = [], []
        for j in range(groups):
            window = wide[pl.ds(top, 16), 16 * j : 16 * j + 16, :].reshape(256, 256)
            fixed = fixed_ref[pl.ds(top, 8), 16 * j : 16 * j + 16, :].reshape(128, 128)
            flow_row, flow_col = tile_flow(window, fixed, prior)
            flow_rows.append(flow_row)
            flow_cols.append(flow_col)
        out_ref[0, g] = jnp.concatenate(flow_rows, axis=0)
        out_ref[1, g] = jnp.concatenate(flow_cols, axis=0)
        return carry

    lax.fori_loop(0, rows // 8, group, 0)


def pair_flow(fixed, low, moving, high, fixed_all, moving_all):
    rows, cols, depth = fixed.shape
    spec = pl.BlockSpec(memory_space=pltpu.VMEM)
    return pl.pallas_call(
        pair_kernel,
        out_shape=jax.ShapeDtypeStruct((2, rows // 8, cols // 16, 128), jnp.float32),
        in_specs=[spec] * 6,
        out_specs=spec,
        scratch_shapes=[
            pltpu.VMEM((rows + 2 * WIN, cols, 2 * depth), jnp.bfloat16),
            pltpu.VMEM((256, 128), jnp.float32),
        ],
        compiler_params=pltpu.CompilerParams(vmem_limit_bytes=40 * 2**20),
        cost_estimate=pl.CostEstimate(
            flops=2 * 256 * 256 * rows * cols, bytes_accessed=2**22, transcendentals=256 * rows * cols
        ),
    )(fixed, low, moving, high, fixed_all, moving_all)


def pool_block(block):
    count, height, width, depth = block.shape
    summed = jnp.sum(
        block.reshape(count, height // POOL, POOL, width // POOL, POOL, depth),
        axis=(2, 4),
        dtype=jnp.float32,
    )
    return (summed / (POOL * POOL)).astype(jnp.bfloat16)


def body(descriptors, partner_step):
    sections, row_count, col_count, depth = descriptors.shape
    sec_index = lax.axis_index("sec")
    first_sec = sec_index * sections
    own_steps = lax.dynamic_slice_in_dim(partner_step, first_sec, sections)
    prev_start = jnp.maximum(first_sec - sections, 0)
    prev_steps = lax.dynamic_slice_in_dim(partner_step, prev_start, sections)
    reach = prev_start + jnp.arange(sections, dtype=jnp.int32) + prev_steps - first_sec
    crossing = (sec_index > 0) & (prev_steps > 0) & (reach >= 0)
    chosen = jnp.sum(jnp.where(crossing, reach, 0))
    sender = jnp.where(own_steps[1] > 0, 1, 0)

    sec_count, tile_count = lax.axis_size("sec"), lax.axis_size("tile")
    back = [(i, i - 1) for i in range(1, sec_count)]
    up = [(i, i + 1) for i in range(tile_count - 1)]
    down = [(b, a) for a, b in up]
    pick = lambda a, k: jnp.where(k == 0, a[0], a[1])
    outgoing = pick(descriptors, chosen)
    incoming = lax.ppermute(outgoing, "sec", back)
    coarse = lax.all_gather(pool_block(descriptors), "tile", axis=1, tiled=True)
    low = lax.ppermute(descriptors[:, row_count - WIN :], "tile", up)
    high = lax.ppermute(descriptors[:, :WIN], "tile", down)
    edges = lax.ppermute(jnp.concatenate([pick(low, chosen), pick(high, chosen)]), "sec", back)
    coarse_in = lax.ppermute(pick(coarse, chosen), "sec", back)
    widen = lambda a: jnp.pad(a, ((WIN, 12 - WIN), (0, BAND - a.shape[1]), (0, 0)))

    near = pair_flow(descriptors[0], low[1], descriptors[1], high[1], coarse[0], widen(coarse[1]))
    far = pair_flow(
        pick(descriptors, sender), edges[:WIN], incoming, edges[WIN:], pick(coarse, sender), widen(coarse_in)
    )
    flow = jnp.stack(
        [
            jnp.where(own_steps[0] == 1, near, jnp.where(own_steps[0] == 2, far, 0.0)),
            jnp.where(own_steps[1] > 0, far, 0.0),
        ]
    )
    flow = flow.reshape(sections, 2, row_count // 8, col_count // 16, 8, 16)
    return flow.transpose(0, 1, 2, 4, 3, 5).reshape(sections, 2, row_count, col_count)


def solution(mesh):
    return jax.shard_map(
        body,
        mesh=mesh,
        in_specs=(P("sec", "tile", None, None), P()),
        out_specs=P("sec", None, "tile", None),
        check_vma=False,
    )
```

profile of v0, /device:TPU:1, one launch (start us, length us, event | category | flops | bytes accessed | tf_op | source)
XLA Modules:
  0.0 55.7 jit_solution(12497102451679750196)
XLA Ops:
  0.0 1.1 %fusion.3 = (bf16[2,4,128,128]{3,2,1,0:T(8,128)(2,1)S(1)}, bf16[2,4,128,128]{3,2,1,0:T(8,128)(2,1)S(1)}) fusion(bf16[2,48,128,128]{3,2,1,0:T(8,128)(2,1)} %param.2), kind=kLoop, calls=%fused_computation.22 | loop fusion | bytes 1048576 | tf_op jit(solution)/shard_map/slice | solution.py:176
  1.1 4.0 %collective-permute-start = (bf16[2,4,128,128]{3,2,1,0:T(8,128)(2,1)S(1)}, bf16[2,4,128,128]{3,2,1,0:T(8,128)(2,1)S(1)}, u32[]{:S(2)}, u32[]{:S(2)}) collective-permute-start(bf16[2,4,128,128]{3,2,1,0:T(8,128)(2,1)S(1)} %get-tuple-element.9), channel_id=1, source_target_pairs={{0,1},{1,2},{2,3},{4,5},{5,6},{6,7},{8,9},{9,10},{10,11},{12,13},{... | collective-permute-start | bytes 786440 | tf_op jit(solution)/shard_map/ppermute | solution.py:176
  5.1 1.3 %collective-permute-start.1 = (bf16[2,4,128,128]{3,2,1,0:T(8,128)(2,1)S(1)}, bf16[2,4,128,128]{3,2,1,0:T(8,128)(2,1)S(1)}, u32[]{:S(2)}, u32[]{:S(2)}) collective-permute-start(bf16[2,4,128,128]{3,2,1,0:T(8,128)(2,1)S(1)} %get-tuple-element.10), channel_id=1, source_target_pairs={{1,0},{2,1},{3,2},{5,4},{6,5},{7,6},{9,8},{10,9},{11,10},{13,12},{... | collective-permute-start | bytes 786440 | tf_op jit(solution)/shard_map/ppermute | solution.py:177
  6.4 1.4 %fusion.2 = (s32[]{:T(128)}, s32[2]{0:T(128)S(1)}) fusion(s32[16]{0:T(128)} %param.3, s32[]{:T(128)S(6)} %max.3, pred[]{:T(512)S(6)} %gt.15, s32[]{:T(128)S(6)} %mul.3, s32[]{:T(128)S(6)} %select_n.78), kind=kLoop, calls=%fused_computation.21 | loop fusion | flops 17 | bytes 2588 | tf_op jit(solution)/shard_map/reduce_sum | solution.py:165
  8.5 0.6 %fusion.5 = (s32[1]{0:T(128)}, s32[1]{0:T(128)}) fusion(s32[2]{0:T(128)S(1)} %get-tuple-element.22), kind=kLoop, calls=%fused_computation.24 | loop fusion | bytes 16 | tf_op jit(solution)/shard_map/slice | solution.py:188
  9.8 0.0 copy-start
  9.8 2.2 %broadcast_select_fusion = (bf16[48,128,128]{2,1,0:T(8,128)(2,1)S(1)}, bf16[48,128,128]{2,1,0:T(8,128)(2,1)S(1)}) fusion(pred[]{:T(512)S(6)} %eq.27, bf16[2,48,128,128]{3,2,1,0:T(8,128)(2,1)} %param.2, pred[]{:T(512)S(6)} %eq.26), kind=kLoop, calls=%fused_computation.3 | loop fusion | flops 1572864 | bytes 6291458 | tf_op jit(solution)/shard_map/jit(_where)/select_n | solution.py:172
  12.0 2.9 %collective-permute-start.3 = (bf16[48,128,128]{2,1,0:T(8,128)(2,1)S(1)}, bf16[48,128,128]{2,1,0:T(8,128)(2,1)S(1)}, u32[]{:S(2)}, u32[]{:S(2)}) collective-permute-start(bf16[48,128,128]{2,1,0:T(8,128)(2,1)S(1)} %get-tuple-element.7), channel_id=1, source_target_pairs={{4,0},{8,4},{12,8},{16,12},{20,16},{24,20},{28,24},{5,1},{9,5},{13... | collective-permute-start | bytes 4718600 | tf_op jit(solution)/shard_map/ppermute | solution.py:174
  14.9 0.0 copy-done
  14.9 0.7 %convert_reduce_fusion = f32[2,6,16,128]{3,2,1,0:T(8,128)S(1)} fusion(bf16[2,6,8,16,8,128]{5,4,3,2,1,0:T(8,128)(2,1)S(1)} %bitcast.53), kind=kLoop, calls=%fused_computation | loop fusion | flops 3121152 | bytes 3244032 | tf_op jit(solution)/shard_map/reduce_sum | solution.py:148
  15.6 13.0 %all_gather.3 = bf16[2,24,16,128]{3,2,1,0:T(8,128)(2,1)S(1)} all-gather(bf16[2,6,16,128]{3,2,1,0:T(8,128)(2,1)S(1)} %multiply_convert_fusion), channel_id=1, replica_groups=mesh['sec'=8,'tile'=4] {'tile'}, dimensions={1}, use_global_device_ids=true | all-gather | bytes 245760 | tf_op jit(solution)/shard_map/all_gather | solution.py:175
  28.6 3.5 %collective-permute-start.4 = (bf16[24,16,128]{2,1,0:T(8,128)(2,1)S(1)}, bf16[24,16,128]{2,1,0:T(8,128)(2,1)S(1)}, u32[]{:S(2)}, u32[]{:S(2)}) collective-permute-start(bf16[24,16,128]{2,1,0:T(8,128)(2,1)S(1)} %get-tuple-element.15), channel_id=1, source_target_pairs={{4,0},{8,4},{12,8},{16,12},{20,16},{24,20},{28,24},{5,1},{9,5},{13... | collective-permute-start | bytes 294920 | tf_op jit(solution)/shard_map/ppermute | solution.py:179
  32.1 0.4 slice_bitcast_fusion
  33.8 2.0 %collective-permute-done.4 = bf16[24,16,128]{2,1,0:T(8,128)(2,1)S(1)} collective-permute-done((bf16[24,16,128]{2,1,0:T(8,128)(2,1)S(1)}, bf16[24,16,128]{2,1,0:T(8,128)(2,1)S(1)}, u32[]{:S(2)}, u32[]{:S(2)}) %collective-permute-start.4) | collective-permute-done | bytes 98336 | tf_op jit(solution)/shard_map/ppermute | solution.py:179
  35.9 0.0 collective-permute-done.1
  36.0 0.0 collective-permute-done
  36.0 1.9 %collective-permute-start.2 = (bf16[8,128,128]{2,1,0:T(8,128)(2,1)S(1)}, bf16[8,128,128]{2,1,0:T(8,128)(2,1)S(1)}, u32[]{:S(2)}, u32[]{:S(2)}) collective-permute-start(bf16[8,128,128]{2,1,0:T(8,128)(2,1)S(1)} %pad_maximum_fusion), channel_id=1, source_target_pairs={{4,0},{8,4},{12,8},{16,12},{20,16},{24,20},{28,24},{5,1},{9,5},{13... | collective-permute-start | bytes 786440 | tf_op jit(solution)/shard_map/ppermute | solution.py:178
  38.0 8.1 %shard_map.28 = f32[2,6,8,128]{3,2,1,0:T(8,128)S(1)} custom-call(bf16[48,128,128]{2,1,0:T(8,128)(2,1)S(1)} %get-tuple-element.6.fixed_ref, bf16[4,128,128]{2,1,0:T(8,128)(2,1)S(1)} %slice_bitcast_fusion.5.low_ref, bf16[48,128,128]{2,1,0:T(8,128)(2,1)S(1)} %get-tuple-element.5.moving_ref, bf16[4,128,128]{2,1,0:T(8,128)(2,1)S(1)} %slice_bitcast_fusion.4.high_ref, ...), custom_call_target="tpu_custom_call" | custom-call | flops 805306368 | bytes 4194304 | tf_op jit(solution)/shard_map/pallas_call | solution.py:130
  46.1 0.0 collective-permute-done.2
  46.1 0.0 collective-permute-done.3.moving_ref
  46.1 8.1 %shard_map.29 = f32[2,6,8,128]{3,2,1,0:T(8,128)S(1)} custom-call(bf16[48,128,128]{2,1,0:T(8,128)(2,1)S(1)} %get-tuple-element.8.fixed_ref, bf16[4,128,128]{2,1,0:T(8,128)(2,1)S(1)} %get-tuple-element.12.low_ref, bf16[48,128,128]{2,1,0:T(8,128)(2,1)S(1)} %collective-permute-done.3.moving_ref, bf16[4,128,128]{2,1,0:T(8,128)(2,1)S(1)} %get-tuple-element.11.high_ref, ...), custom_call_target="tpu_custom_call" | custom-call | flops 805306368 | bytes 4194304 | tf_op jit(solution)/shard_map/pallas_call | solution.py:130
  54.2 0.2 stack.10
  54.4 0.2 stack.9
  54.5 0.1 maximum_bitcast_fusion
  54.6 0.1 copy.3
  54.8 0.9 %reshape.17 = f32[2,2,48,128]{3,2,1,0:T(8,128)} reshape(f32[2,2,6,8,8,16]{5,4,3,2,1,0:T(8,128)S(1)} %copy.3) | data formatting | bytes 196608 | tf_op jit(solution)/shard_map/reshape | solution.py:193
  (12 shorter events, 0.2 us)
Async XLA Ops:
  1.1 34.9 %collective-permute-start = (bf16[2,4,128,128]{3,2,1,0:T(8,128)(2,1)S(1)}, bf16[2,4,128,128]{3,2,1,0:T(8,128)(2,1)S(1)}, u32[]{:S(2)}, u32[]{:S(2)}) collective-permute-start(bf16[2,4,128,128]{3,2,1,0:T(8,128)(2,1)S(1)} %get-tuple-element.9), channel_id=1, source_target_pairs={{0,1},{1,2},{2,3},{4,5},{5,6},{6,7},{8,9},{9,10},{10,11},{12,13},{... | collective-permute-start | bytes 786440 | tf_op jit(solution)/shard_map/ppermute | solution.py:176
  5.1 30.8 %collective-permute-start.1 = (bf16[2,4,128,128]{3,2,1,0:T(8,128)(2,1)S(1)}, bf16[2,4,128,128]{3,2,1,0:T(8,128)(2,1)S(1)}, u32[]{:S(2)}, u32[]{:S(2)}) collective-permute-start(bf16[2,4,128,128]{3,2,1,0:T(8,128)(2,1)S(1)} %get-tuple-element.10), channel_id=1, source_target_pairs={{1,0},{2,1},{3,2},{5,4},{6,5},{7,6},{9,8},{10,9},{11,10},{13,12},{... | collective-permute-start | bytes 786440 | tf_op jit(solution)/shard_map/ppermute | solution.py:177
  9.8 5.1 %copy-start = (bf16[2,48,128,128]{3,2,1,0:T(8,128)(2,1)S(1)}, bf16[2,48,128,128]{3,2,1,0:T(8,128)(2,1)}, u32[]{:S(2)}) copy-start(bf16[2,48,128,128]{3,2,1,0:T(8,128)(2,1)} %param.2) | copy-start | bytes 9437188
  12.0 34.1 %collective-permute-start.3 = (bf16[48,128,128]{2,1,0:T(8,128)(2,1)S(1)}, bf16[48,128,128]{2,1,0:T(8,128)(2,1)S(1)}, u32[]{:S(2)}, u32[]{:S(2)}) collective-permute-start(bf16[48,128,128]{2,1,0:T(8,128)(2,1)S(1)} %get-tuple-element.7), channel_id=1, source_target_pairs={{4,0},{8,4},{12,8},{16,12},{20,16},{24,20},{28,24},{5,1},{9,5},{13... | collective-permute-start | bytes 4718600 | tf_op jit(solution)/shard_map/ppermute | solution.py:174
  28.6 7.3 %collective-permute-start.4 = (bf16[24,16,128]{2,1,0:T(8,128)(2,1)S(1)}, bf16[24,16,128]{2,1,0:T(8,128)(2,1)S(1)}, u32[]{:S(2)}, u32[]{:S(2)}) collective-permute-start(bf16[24,16,128]{2,1,0:T(8,128)(2,1)S(1)} %get-tuple-element.15), channel_id=1, source_target_pairs={{4,0},{8,4},{12,8},{16,12},{20,16},{24,20},{28,24},{5,1},{9,5},{13... | collective-permute-start | bytes 294920 | tf_op jit(solution)/shard_map/ppermute | solution.py:179
  36.0 10.0 %collective-permute-start.2 = (bf16[8,128,128]{2,1,0:T(8,128)(2,1)S(1)}, bf16[8,128,128]{2,1,0:T(8,128)(2,1)S(1)}, u32[]{:S(2)}, u32[]{:S(2)}) collective-permute-start(bf16[8,128,128]{2,1,0:T(8,128)(2,1)S(1)} %pad_maximum_fusion), channel_id=1, source_target_pairs={{4,0},{8,4},{12,8},{16,12},{20,16},{24,20},{28,24},{5,1},{9,5},{13... | collective-permute-start | bytes 786440 | tf_op jit(solution)/shard_map/ppermute | solution.py:178
where the time goes:
time: 56.6 us; the launch traced here: 55.7 us
  Pallas kernels  16.1 us (28%)
  starting transfers between devices  13.6 us (24%)
  blocking collectives  13 us (23%)
  other arithmetic  4.56 us (8%)
  local copies, waits for them, and re-layouts  3.51 us (6%)
  between operations  2.84 us (5%)
  waiting for transfers between devices  2.06 us (4%)
    pallas_call x2, Pallas kernels, pair_flow(): pl.pallas_call(pair_kernel, out_shape=jax.ShapeDtypeStruct((2, rows // 8,...  16.1 us
    all_gather x1, blocking collectives, body(): coarse = lax.all_gather(pool_block(descriptors), 'tile', axis=1, tiled=True)  13 us
    ppermute x1, starting transfers between devices, body(): low = lax.ppermute(descriptors[:, row_count - WIN:], 'tile', up)  4.05 us
    ppermute x1, starting transfers between devices, body(): coarse_in = lax.ppermute(pick(coarse, chosen), 'sec', back)  3.49 us
    ppermute x1, starting transfers between devices, body(): incoming = lax.ppermute(outgoing, 'sec', back)  2.86 us
    select_n x4, other arithmetic, body(): pick = lambda a, k: jnp.where(k == 0, a[0], a[1])  2.29 us
    ppermute x1, waiting for transfers between devices, body(): coarse_in = lax.ppermute(pick(coarse, chosen), 'sec', back)  2.04 us
    ppermute x1, starting transfers between devices, body(): lax.ppermute(jnp.concatenate([pick(low, chosen), pick(high, chosen)]), 's...  1.92 us
  transfers between devices with their start and end apart: 5, of which 1 were waited for; matrix products, arithmetic and copies ran while one was open for 10% of the time, Pallas kernels for 14%

commit v1 on v0

v1 whole, which is shorter than its diff:
```python
import functools
import math

import jax
import jax.numpy as jnp
from jax import lax
from jax.experimental import pallas as pl
from jax.experimental.pallas import tpu as pltpu
from jax.sharding import PartitionSpec as P

WIN = 4
POOL = 8
SIDE = 2 * WIN + 1
PRIOR = 0.25
LOG2E = math.log2(math.e)
BAND = 32
LOW = -1e30


def coarse_shift(fixed_row, padded_ref, count):
    cols, depth = 16, padded_ref.shape[2]
    lanes = 12 * BAND

    def step(y, total):
        window = padded_ref[pl.ds(y, 12)].reshape(lanes, depth)
        return total + lax.dot_general(
            fixed_row(y), window, (((1,), (1,)), ((), ())), preferred_element_type=jnp.float32
        )

    table = lax.fori_loop(0, count, step, jnp.zeros((cols, lanes), jnp.float32))
    row = lax.broadcasted_iota(jnp.int32, (cols, lanes), 0)
    for bit in (1, 2, 4, 8):
        table = jnp.where((row & bit) != 0, pltpu.roll(table, lanes - bit, 1), table)
    scores = jnp.sum(table, axis=0, keepdims=True) * (
        1.0 / math.sqrt(depth * count * cols)
    )
    lane = lax.broadcasted_iota(jnp.int32, (1, lanes), 1) + BAND // 2
    lane = jnp.where(lane >= lanes, lane - lanes, lane)
    dy = (lane // BAND) - WIN
    dx = (lane % BAND) - BAND // 2
    valid = (dy <= WIN) & (jnp.abs(dx) <= WIN)
    scores = jnp.where(valid, scores, LOW)
    weights = jnp.exp(scores - jnp.max(scores, axis=1, keepdims=True))
    total = jnp.sum(weights, axis=1, keepdims=True)
    return (
        jnp.sum(weights * dy.astype(jnp.float32), axis=1, keepdims=True) / total,
        jnp.sum(weights * dx.astype(jnp.float32), axis=1, keepdims=True) / total,
    )


def fill_prior(prior_ref, shift_row, shift_col):
    shape = (256, 128)
    at = lax.broadcasted_iota(jnp.int32, shape, 0)
    cell = lax.broadcasted_iota(jnp.int32, shape, 1)
    dy = (at // 16) - (cell // 16) - WIN
    dx = (at % 16) - (cell % 8) - WIN
    valid = (jnp.abs(dy) <= WIN) & (jnp.abs(dx) <= WIN)
    far = (dy.astype(jnp.float32) - shift_row) ** 2 + (dx.astype(jnp.float32) - shift_col) ** 2
    prior_ref[...] = jnp.where(valid, far * (-PRIOR * LOG2E), LOW)


def widen_row(wide_ref, at, row):
    row = row.astype(jnp.float32)
    edge = jnp.zeros((WIN, row.shape[1]), jnp.float32)
    left = jnp.concatenate([edge, row[:-WIN]], axis=0)
    right = jnp.concatenate([row[WIN:], edge], axis=0)
    wide_ref[at] = jnp.concatenate([left, right], axis=1).astype(jnp.bfloat16)


def tile_flow(window, fixed, prior_ref):
    cell = lax.broadcasted_iota(jnp.int32, fixed.shape, 0)
    first = ((cell % 16) < 8).astype(jnp.float32).astype(jnp.bfloat16)
    both = jnp.concatenate([fixed * first, fixed * (jnp.bfloat16(1.0) - first)], axis=1)
    corr = lax.dot_general(
        window, both, (((1,), (1,)), ((), ())), preferred_element_type=jnp.float32
    )
    scores = corr * (LOG2E / math.sqrt(fixed.shape[1])) + prior_ref[...]
    weights = jnp.exp2(scores - jnp.max(scores, axis=0, keepdims=True)).reshape(16, 16, 128)
    down = weights[15]
    rows = down
    for at in range(14, 0, -1):
        down = down + weights[at]
        rows = rows + down
    down = down + weights[0]
    inverse = 1.0 / jnp.sum(down, axis=0, keepdims=True)
    at = lax.broadcasted_iota(jnp.int32, (16, 128), 0).astype(jnp.float32)
    cell = lax.broadcasted_iota(jnp.int32, (1, 128), 1)
    flow_row = jnp.sum(rows, axis=0, keepdims=True) * inverse
    flow_col = jnp.sum(down * at, axis=0, keepdims=True) * inverse
    return (
        flow_row - ((cell // 16) + WIN).astype(jnp.float32),
        flow_col - ((cell % 8) + WIN).astype(jnp.float32),
    )


def flow_group(wide, fixed_rows, prior, out_ref, g):
    flow_rows, flow_cols = [], []
    top = pl.multiple_of(g * 8, 8)
    for j in range(wide.shape[1] // 16):
        window = wide[pl.ds(top, 16), 16 * j : 16 * j + 16, :].reshape(256, 256)
        fixed = fixed_rows(top, 16 * j).reshape(128, 128)
        flow_row, flow_col = tile_flow(window, fixed, prior)
        flow_rows.append(flow_row)
        flow_cols.append(flow_col)
    out_ref[0, g] = jnp.concatenate(flow_rows, axis=0)
    out_ref[1, g] = jnp.concatenate(flow_cols, axis=0)


def loop(start, stop, step):
    def run(at, carry):
        step(at)
        return carry

    lax.fori_loop(start, stop, run, 0)


def kernel(
    secs, tiles, desc, steps, out,
    sending, incoming, coarse, coarse_out, coarse_in, padded, near_edge, far_edge, wide, prior, near, far,
    main_send, main_recv, near_send, near_recv, far_send, far_recv,
    gather_send, gather_recv, hop_send, hop_recv, spread_send, spread_recv,
):
    rows = desc.shape[1]
    chunks = rows // POOL
    i, t = lax.axis_index("sec"), lax.axis_index("tile")
    own_first, own_second = steps[2 * i], steps[2 * i + 1]
    chosen = jnp.where(steps[jnp.maximum(2 * i - 1, 0)] == 2, 1, 0)
    sender = jnp.where(own_second > 0, 1, 0)
    gives, takes = i > 0, i < secs - 1

    def peer(d):
        return lax.rem(t + d, tiles)

    def remote(src, dst, send, recv, target):
        return pltpu.make_async_remote_copy(
            src_ref=src, dst_ref=dst, send_sem=send, recv_sem=recv,
            device_id=target, device_id_type=pl.DeviceIdType.MESH,
        )

    def main_copy(k):
        part = pl.ds(pl.multiple_of(k * POOL, POOL), POOL)
        return remote(
            sending.at[part], incoming.at[part], main_send.at[k], main_recv.at[k], {"sec": i - 1}
        )

    def gather_copy(d):
        slot = coarse.at[:, t]
        return remote(slot, slot, gather_send.at[d], gather_recv.at[d], {"tile": peer(d)})

    def hop_copy():
        return remote(coarse_out, coarse_in.at[t], hop_send, hop_recv, {"sec": i - 1})

    def spread_copy(d):
        slot = coarse_in.at[t]
        return remote(slot, slot, spread_send.at[d], spread_recv.at[d], {"tile": peer(d)})

    def edge_copy(source, edge, sems, side):
        part = source.at[rows - WIN :] if side == 0 else source.at[:WIN]
        target = t + 1 if side == 0 else t - 1
        return remote(part, edge.at[side], sems[0].at[side], sems[1].at[side], {"tile": target})

    near_sems, far_sems = (near_send, near_recv), (far_send, far_recv)
    near_source = desc.at[1]
    has_low, has_high = t > 0, t < tiles - 1

    def start_edges(source, edge, sems):
        pl.when(has_high)(lambda: edge_copy(source, edge, sems, 0).start())
        pl.when(has_low)(lambda: edge_copy(source, edge, sems, 1).start())

    def finish_edges(source, edge, sems):
        pl.when(has_high)(lambda: edge_copy(source, edge, sems, 0).wait_send())
        pl.when(has_low)(lambda: edge_copy(source, edge, sems, 1).wait_send())

    def receive_edges(source, edge, sems):
        pl.when(has_low)(lambda: edge_copy(source, edge, sems, 0).wait_recv())
        pl.when(has_high)(lambda: edge_copy(source, edge, sems, 1).wait_recv())

        @pl.when(t == 0)
        def _():
            edge[0] = jnp.zeros(edge.shape[1:], edge.dtype)

        @pl.when(t == tiles - 1)
        def _():
            edge[1] = jnp.zeros(edge.shape[1:], edge.dtype)

        for r in range(WIN):
            widen_row(wide, r, edge[0, r])
            widen_row(wide, rows + WIN + r, edge[1, r])

    barrier = pltpu.get_barrier_semaphore()

    def greet(target):
        pl.semaphore_signal(barrier, inc=1, device_id=target, device_id_type=pl.DeviceIdType.MESH)

    for d in range(1, tiles):
        greet({"tile": peer(d)})
    pl.when(gives)(lambda: greet({"sec": i - 1}))
    pl.when(takes)(lambda: greet({"sec": i + 1}))

    def fill(r):
        sending[r] = desc[chosen, r]

    loop(0, rows, fill)
    pl.semaphore_wait(barrier, tiles - 1 + jnp.where(gives, 1, 0) + jnp.where(takes, 1, 0))

    @pl.when(gives)
    def _():
        main_copy(0).start()
        main_copy(chunks - 1).start()

    start_edges(near_source, near_edge, near_sems)

    def pool(k):
        means = []
        for s in range(2):
            summed = desc[s, k * POOL].astype(jnp.float32)
            for r in range(1, POOL):
                summed = summed + desc[s, k * POOL + r].astype(jnp.float32)
            summed = jnp.sum(summed.reshape(16, POOL, summed.shape[1]), axis=1)
            means.append(summed * (1.0 / (POOL * POOL)))
            coarse[s, t, k] = means[s].astype(jnp.bfloat16)
        coarse_out[k] = jnp.where(chosen == 0, means[0], means[1]).astype(jnp.bfloat16)

    loop(0, chunks, pool)
    for d in range(1, tiles):
        gather_copy(d).start()

    @pl.when(gives)
    def _():
        hop_copy().start()
        loop(1, chunks - 1, lambda k: main_copy(k).start())

    total = tiles * chunks
    padded[...] = jnp.zeros(padded.shape, padded.dtype)
    loop(0, rows, lambda r: widen_row(wide, r + WIN, desc[1, r]))
    for d in range(1, tiles):
        gather_copy(d).wait_recv()

    def lay(load):
        for at in range(tiles):
            for k in range(chunks):
                padded[WIN + at * chunks + k, :16] = load(at, k)

    lay(lambda at, k: coarse[1, at, k])
    shift_row, shift_col = coarse_shift(lambda y: coarse[0, y // chunks, y % chunks], padded, total)
    fill_prior(prior, shift_row, shift_col)
    receive_edges(near_source, near_edge, near_sems)
    loop(
        0, chunks,
        lambda g: flow_group(wide, lambda top, col: desc[0, pl.ds(top, 8), col : col + 16, :], prior, near, g),
    )

    @pl.when(takes)
    def _():
        hop_copy().wait_recv()
        for d in range(1, tiles):
            spread_copy(d).start()
        main_copy(0).wait_recv()
        main_copy(chunks - 1).wait_recv()
        start_edges(incoming, far_edge, far_sems)
        for r in range(POOL):
            widen_row(wide, r + WIN, incoming[r])
            widen_row(wide, rows - POOL + r + WIN, incoming[rows - POOL + r])
        for d in range(1, tiles):
            spread_copy(d).wait_recv()
        lay(lambda at, k: coarse_in[at, k])
        shift_row, shift_col = coarse_shift(lambda y: coarse[sender, y // chunks, y % chunks], padded, total)
        fill_prior(prior, shift_row, shift_col)
        receive_edges(incoming, far_edge, far_sems)

        def group(g):
            @pl.when(g < chunks - 2)
            def _():
                main_copy(g + 1).wait_recv()
                first = (g + 1) * POOL
                for r in range(POOL):
                    widen_row(wide, first + r + WIN, incoming[first + r])

            flow_group(wide, lambda top, col: desc[sender, pl.ds(top, 8), col : col + 16, :], prior, far, g)

        loop(0, chunks, group)
        for d in range(1, tiles):
            spread_copy(d).wait_send()
        finish_edges(incoming, far_edge, far_sems)

    @pl.when(i == secs - 1)
    def _():
        far[...] = jnp.zeros(far.shape, far.dtype)

    for c in range(2):
        out[0, c] = jnp.where(own_first == 1, near[c], jnp.where(own_first == 2, far[c], 0.0))
        out[1, c] = jnp.where(own_second > 0, far[c], 0.0)

    for d in range(1, tiles):
        gather_copy(d).wait_send()
    finish_edges(near_source, near_edge, near_sems)

    @pl.when(gives)
    def _():
        hop_copy().wait_send()
        loop(0, chunks, lambda k: main_copy(k).wait_send())


def body(descriptors, partner_step):
    sections, rows, cols, depth = descriptors.shape
    secs, tiles = lax.axis_size("sec"), lax.axis_size("tile")
    chunks = rows // POOL
    narrow = jnp.bfloat16
    dma = pltpu.SemaphoreType.DMA
    result = (2, chunks, cols // 16, 128)
    flow = pl.pallas_call(
        functools.partial(kernel, secs, tiles),
        out_shape=jax.ShapeDtypeStruct((sections,) + result, jnp.float32),
        in_specs=[pl.BlockSpec(memory_space=pltpu.VMEM), pl.BlockSpec(memory_space=pltpu.SMEM)],
        out_specs=pl.BlockSpec(memory_space=pltpu.VMEM),
        scratch_shapes=[
            pltpu.VMEM((rows, cols, depth), narrow),
            pltpu.VMEM((rows, cols, depth), narrow),
            pltpu.VMEM((sections, tiles, chunks, 16, depth), narrow),
            pltpu.VMEM((chunks, 16, depth), narrow),
            pltpu.VMEM((tiles, chunks, 16, depth), narrow),
            pltpu.VMEM((tiles * chunks + 12, BAND, depth), narrow),
            pltpu.VMEM((2, WIN, cols, depth), narrow),
            pltpu.VMEM((2, WIN, cols, depth), narrow),
            pltpu.VMEM((rows + 2 * WIN, cols, 2 * depth), narrow),
            pltpu.VMEM((256, 128), jnp.float32),
            pltpu.VMEM(result, jnp.float32),
            pltpu.VMEM(result, jnp.float32),
            dma((chunks,)), dma((chunks,)), dma((2,)), dma((2,)), dma((2,)), dma((2,)),
            dma((tiles,)), dma((tiles,)), dma, dma, dma((tiles,)), dma((tiles,)),
        ],
        compiler_params=pltpu.CompilerParams(
            vmem_limit_bytes=40 * 2**20, collective_id=0, has_side_effects=True
        ),
        cost_estimate=pl.CostEstimate(
            flops=4 * 256 * 256 * rows * cols, bytes_accessed=2**22, transcendentals=512 * rows * cols
        ),
    )(descriptors, partner_step)
    flow = flow.reshape(sections, 2, chunks, cols // 16, 8, 16)
    return flow.transpose(0, 1, 2, 4, 3, 5).reshape(sections, 2, rows, cols)


def solution(mesh):
    return jax.shard_map(
        body,
        mesh=mesh,
        in_specs=(P("sec", "tile", None, None), P()),
        out_specs=P("sec", None, "tile", None),
        check_vma=False,
    )
```

time: 56.6 us -> 37.7 us (0.67)
  the two profiles are of different devices: /device:TPU:1 before, /device:TPU:0 now
where the time goes in v1:
time: 37.7 us; the launch traced here: 37.6 us
  Pallas kernels  33.7 us (89%)
  local copies, waits for them, and re-layouts  3.82 us (10%)
    pallas_call x1, Pallas kernels, body(): pl.pallas_call(functools.partial(kernel, secs, tiles), out_shape=jax.Shap...  33.7 us
    unnamed x4, local copies, waits for them, and re-layouts  2.54 us
    reshape x1, local copies, waits for them, and re-layouts, body(): return flow.transpose(0, 1, 2, 4, 3, 5).reshape(sections, 2, rows, cols)  0.89 us

profile of v1, /device:TPU:0, one launch (start us, length us, event | category | flops | bytes accessed | tf_op | source)
XLA Modules:
  0.0 37.6 jit_solution(4724830284623571483)
XLA Ops:
  0.0 0.0 copy-start
  0.0 1.9 %copy-done = bf16[2,48,128,128]{3,2,1,0:T(8,128)(2,1)S(1)} copy-done((bf16[2,48,128,128]{3,2,1,0:T(8,128)(2,1)S(1)}, bf16[2,48,128,128]{3,2,1,0:T(8,128)(2,1)}, u32[]{:S(2)}) %copy-start) | copy-done | bytes 3145752
  1.9 0.0 copy-start.1
  1.9 0.7 %copy-done.1 = s32[16]{0:T(128)S(1)} copy-done((s32[16]{0:T(128)S(1)}, s32[16]{0:T(128)}, u32[]{:S(2)}) %copy-start.1) | copy-done | bytes 88
  2.5 33.7 %shard_map.28 = f32[2,2,6,8,128]{4,3,2,1,0:T(8,128)S(1)} custom-call(bf16[2,48,128,128]{3,2,1,0:T(8,128)(2,1)S(1)} %copy-done, s32[16]{0:T(128)S(1)} %copy-done.1), custom_call_target="tpu_custom_call" | custom-call | flops 1610612736 | bytes 4194304 | tf_op jit(solution)/shard_map/pallas_call | solution.py:311
  36.3 0.2 reshape.6
  36.5 0.1 copy.3
  36.7 0.9 %reshape.7 = f32[2,2,48,128]{3,2,1,0:T(8,128)} reshape(f32[2,2,6,8,8,16]{5,4,3,2,1,0:T(8,128)S(1)} %copy.3) | data formatting | bytes 196608 | tf_op jit(solution)/shard_map/reshape | solution.py:340
Async XLA Ops:
  0.0 1.9 %copy-start = (bf16[2,48,128,128]{3,2,1,0:T(8,128)(2,1)S(1)}, bf16[2,48,128,128]{3,2,1,0:T(8,128)(2,1)}, u32[]{:S(2)}) copy-start(bf16[2,48,128,128]{3,2,1,0:T(8,128)(2,1)} %desc.1) | copy-start | bytes 9437188
  1.9 0.7 %copy-start.1 = (s32[16]{0:T(128)S(1)}, s32[16]{0:T(128)}, u32[]{:S(2)}) copy-start(s32[16]{0:T(128)} %steps.1) | copy-start | bytes 196

commit v2 on v1

--- a/solution.py
+++ b/solution.py
@@ -13,31 +13,31 @@
 SIDE = 2 * WIN + 1
 PRIOR = 0.25
 LOG2E = math.log2(math.e)
-BAND = 32
 LOW = -1e30
 
 
 def coarse_shift(fixed_row, padded_ref, count):
-    cols, depth = 16, padded_ref.shape[2]
-    lanes = 12 * BAND
-
-    def step(y, total):
-        window = padded_ref[pl.ds(y, 12)].reshape(lanes, depth)
-        return total + lax.dot_general(
-            fixed_row(y), window, (((1,), (1,)), ((), ())), preferred_element_type=jnp.float32
+    cols, depth = padded_ref.shape[1:]
+    lanes = 16 * cols
+    table = jnp.zeros((cols, lanes), jnp.float32)
+    for y in range(0, count, 2):
+        fixed = jnp.concatenate([fixed_row(y), fixed_row(y + 1)], axis=1)
+        window = jnp.concatenate(
+            [padded_ref[y + k : y + k + 16].reshape(lanes, depth) for k in (0, 1)], axis=1
         )
-
-    table = lax.fori_loop(0, count, step, jnp.zeros((cols, lanes), jnp.float32))
+        table = table + lax.dot_general(
+            fixed, window, (((1,), (1,)), ((), ())), preferred_element_type=jnp.float32
+        )
     row = lax.broadcasted_iota(jnp.int32, (cols, lanes), 0)
+    lane = lax.broadcasted_iota(jnp.int32, (cols, lanes), 1)
+    table = jnp.where(jnp.abs(lane % cols - row) <= WIN, table, 0.0)
     for bit in (1, 2, 4, 8):
         table = jnp.where((row & bit) != 0, pltpu.roll(table, lanes - bit, 1), table)
-    scores = jnp.sum(table, axis=0, keepdims=True) * (
-        1.0 / math.sqrt(depth * count * cols)
-    )
-    lane = lax.broadcasted_iota(jnp.int32, (1, lanes), 1) + BAND // 2
+    scores = jnp.sum(table, axis=0, keepdims=True) * (1.0 / math.sqrt(depth * count * cols))
+    lane = lax.broadcasted_iota(jnp.int32, (1, lanes), 1) + cols // 2
     lane = jnp.where(lane >= lanes, lane - lanes, lane)
-    dy = (lane // BAND) - WIN
-    dx = (lane % BAND) - BAND // 2
+    dy = (lane // cols) - WIN
+    dx = (lane % cols) - cols // 2
     valid = (dy <= WIN) & (jnp.abs(dx) <= WIN)
     scores = jnp.where(valid, scores, LOW)
     weights = jnp.exp(scores - jnp.max(scores, axis=1, keepdims=True))
@@ -106,6 +106,17 @@
     out_ref[1, g] = jnp.concatenate(flow_cols, axis=0)
 
 
+def block_transpose(block):
+    row = lax.broadcasted_iota(jnp.int32, block.shape, 0)
+    part = lax.broadcasted_iota(jnp.int32, block.shape, 1) // 16
+    for bit in (1, 2, 4):
+        in_row, in_part = (row & bit) != 0, (part & bit) != 0
+        down = pltpu.roll(pltpu.roll(block, bit, 0), 128 - 16 * bit, 1)
+        up = pltpu.roll(pltpu.roll(block, 8 - bit, 0), 16 * bit, 1)
+        block = jnp.where(in_row == in_part, block, jnp.where(in_row, down, up))
+    return block
+
+
 def loop(start, stop, step):
     def run(at, carry):
         step(at)
@@ -115,18 +126,25 @@
 
 
 def kernel(
-    secs, tiles, desc, steps, out,
-    sending, incoming, coarse, coarse_out, coarse_in, padded, near_edge, far_edge, wide, prior, near, far,
+    secs, tiles, desc_far, steps_far, out,
+    desc, steps, load_sem, steps_sem, sending, incoming, coarse, coarse_out, coarse_in, padded, near_edge, far_edge, wide, prior, near, far,
     main_send, main_recv, near_send, near_recv, far_send, far_recv,
     gather_send, gather_recv, hop_send, hop_recv, spread_send, spread_recv,
 ):
     rows = desc.shape[1]
     chunks = rows // POOL
     i, t = lax.axis_index("sec"), lax.axis_index("tile")
-    own_first, own_second = steps[2 * i], steps[2 * i + 1]
-    chosen = jnp.where(steps[jnp.maximum(2 * i - 1, 0)] == 2, 1, 0)
-    sender = jnp.where(own_second > 0, 1, 0)
     gives, takes = i > 0, i < secs - 1
+
+    def load(k):
+        part = pl.ds(pl.multiple_of(k * POOL, POOL), POOL)
+        return pltpu.make_async_copy(desc_far.at[:, part], desc.at[:, part], load_sem.at[k])
+
+    steps_load = pltpu.make_async_copy(steps_far, steps, steps_sem)
+    steps_load.start()
+    load(0).start()
+    load(chunks - 1).start()
+    loop(1, chunks - 1, lambda k: load(k).start())
 
     def peer(d):
         return lax.rem(t + d, tiles)
@@ -197,10 +215,21 @@
     pl.when(gives)(lambda: greet({"sec": i - 1}))
     pl.when(takes)(lambda: greet({"sec": i + 1}))
 
-    def fill(r):
-        sending[r] = desc[chosen, r]
-
-    loop(0, rows, fill)
+    padded[...] = jnp.zeros(padded.shape, padded.dtype)
+    steps_load.wait()
+    own_first, own_second = steps[2 * i], steps[2 * i + 1]
+    chosen = jnp.where(steps[jnp.maximum(2 * i - 1, 0)] == 2, 1, 0)
+    sender = jnp.where(own_second > 0, 1, 0)
+
+    def fill(k):
+        for r in range(POOL):
+            sending[k * POOL + r] = desc[chosen, k * POOL + r]
+
+    load(0).wait()
+    load(chunks - 1).wait()
+    loop(1, chunks - 1, lambda k: load(k).wait())
+    fill(0)
+    fill(chunks - 1)
     pl.semaphore_wait(barrier, tiles - 1 + jnp.where(gives, 1, 0) + jnp.where(takes, 1, 0))
 
     @pl.when(gives)
@@ -228,23 +257,39 @@
     @pl.when(gives)
     def _():
         hop_copy().start()
-        loop(1, chunks - 1, lambda k: main_copy(k).start())
-
+
+    def pass_on(k):
+        fill(k)
+        pl.when(gives)(lambda: main_copy(k).start())
+
+    loop(1, chunks - 1, pass_on)
     total = tiles * chunks
-    padded[...] = jnp.zeros(padded.shape, padded.dtype)
     loop(0, rows, lambda r: widen_row(wide, r + WIN, desc[1, r]))
     for d in range(1, tiles):
         gather_copy(d).wait_recv()
 
-    def lay(load):
+    @pl.when(takes)
+    def _():
+        hop_copy().wait_recv()
+        for d in range(1, tiles):
+            spread_copy(d).start()
+
+    def lay(entry):
         for at in range(tiles):
             for k in range(chunks):
-                padded[WIN + at * chunks + k, :16] = load(at, k)
+                padded[WIN + at * chunks + k] = entry(at, k)
 
     lay(lambda at, k: coarse[1, at, k])
     shift_row, shift_col = coarse_shift(lambda y: coarse[0, y // chunks, y % chunks], padded, total)
     fill_prior(prior, shift_row, shift_col)
     receive_edges(near_source, near_edge, near_sems)
+
+    @pl.when(takes)
+    def _():
+        main_copy(0).wait_recv()
+        main_copy(chunks - 1).wait_recv()
+        start_edges(incoming, far_edge, far_sems)
+
     loop(
         0, chunks,
         lambda g: flow_group(wide, lambda top, col: desc[0, pl.ds(top, 8), col : col + 16, :], prior, near, g),
@@ -252,12 +297,6 @@
 
     @pl.when(takes)
     def _():
-        hop_copy().wait_recv()
-        for d in range(1, tiles):
-            spread_copy(d).start()
-        main_copy(0).wait_recv()
-        main_copy(chunks - 1).wait_recv()
-        start_edges(incoming, far_edge, far_sems)
         for r in range(POOL):
             widen_row(wide, r + WIN, incoming[r])
             widen_row(wide, rows - POOL + r + WIN, incoming[rows - POOL + r])
@@ -287,10 +326,14 @@
     def _():
         far[...] = jnp.zeros(far.shape, far.dtype)
 
-    for c in range(2):
-        out[0, c] = jnp.where(own_first == 1, near[c], jnp.where(own_first == 2, far[c], 0.0))
-        out[1, c] = jnp.where(own_second > 0, far[c], 0.0)
-
+    def write(g):
+        part = pl.ds(pl.multiple_of(g * POOL, POOL), POOL)
+        for c in range(2):
+            first = jnp.where(own_first == 1, near[c, g], jnp.where(own_first == 2, far[c, g], 0.0))
+            out[0, c, part] = block_transpose(first)
+            out[1, c, part] = block_transpose(jnp.where(own_second > 0, far[c, g], 0.0))
+
+    loop(0, chunks, write)
     for d in range(1, tiles):
         gather_copy(d).wait_send()
     finish_edges(near_source, near_edge, near_sems)
@@ -308,18 +351,21 @@
     narrow = jnp.bfloat16
     dma = pltpu.SemaphoreType.DMA
     result = (2, chunks, cols // 16, 128)
-    flow = pl.pallas_call(
+    return pl.pallas_call(
         functools.partial(kernel, secs, tiles),
-        out_shape=jax.ShapeDtypeStruct((sections,) + result, jnp.float32),
-        in_specs=[pl.BlockSpec(memory_space=pltpu.VMEM), pl.BlockSpec(memory_space=pltpu.SMEM)],
+        out_shape=jax.ShapeDtypeStruct((sections, 2, rows, cols), jnp.float32),
+        in_specs=[pl.BlockSpec(memory_space=pltpu.HBM), pl.BlockSpec(memory_space=pltpu.HBM)],
         out_specs=pl.BlockSpec(memory_space=pltpu.VMEM),
         scratch_shapes=[
+            pltpu.VMEM((sections, rows, cols, depth), narrow),
+            pltpu.SMEM(partner_step.shape, jnp.int32),
+            dma((chunks,)), dma,
             pltpu.VMEM((rows, cols, depth), narrow),
             pltpu.VMEM((rows, cols, depth), narrow),
             pltpu.VMEM((sections, tiles, chunks, 16, depth), narrow),
             pltpu.VMEM((chunks, 16, depth), narrow),
             pltpu.VMEM((tiles, chunks, 16, depth), narrow),
-            pltpu.VMEM((tiles * chunks + 12, BAND, depth), narrow),
+            pltpu.VMEM((tiles * chunks + 16, 16, depth), narrow),
             pltpu.VMEM((2, WIN, cols, depth), narrow),
             pltpu.VMEM((2, WIN, cols, depth), narrow),
             pltpu.VMEM((rows + 2 * WIN, cols, 2 * depth), narrow),
@@ -330,14 +376,12 @@
             dma((tiles,)), dma((tiles,)), dma, dma, dma((tiles,)), dma((tiles,)),
         ],
         compiler_params=pltpu.CompilerParams(
-            vmem_limit_bytes=40 * 2**20, collective_id=0, has_side_effects=True
+            vmem_limit_bytes=52 * 2**20, collective_id=0, has_side_effects=True
         ),
         cost_estimate=pl.CostEstimate(
             flops=4 * 256 * 256 * rows * cols, bytes_accessed=2**22, transcendentals=512 * rows * cols
         ),
     )(descriptors, partner_step)
-    flow = flow.reshape(sections, 2, chunks, cols // 16, 8, 16)
-    return flow.transpose(0, 1, 2, 4, 3, 5).reshape(sections, 2, rows, cols)
 
 
 def solution(mesh):

time: 37.7 us -> 29.5 us (0.78)
  the two profiles are of different devices: /device:TPU:0 before, /device:TPU:1 now
where the time goes in v2:
time: 29.5 us; the launch traced here: 29.4 us
  Pallas kernels  28.1 us (95%)
  local copies, waits for them, and re-layouts  1.3 us (4%)
    pallas_call x1, Pallas kernels, body(): pl.pallas_call(functools.partial(kernel, secs, tiles), out_shape=jax.Shap...  28.1 us
    unnamed x3, local copies, waits for them, and re-layouts  1.3 us

profile of v2, /device:TPU:1, one launch (start us, length us, event | category | flops | bytes accessed | tf_op | source)
XLA Modules:
  0.0 29.4 jit_solution(8464091639656265709)
XLA Ops:
  0.0 0.0 copy-start
  0.0 0.7 %copy-done = s32[16]{0:T(128)S(1)} copy-done((s32[16]{0:T(128)S(1)}, s32[16]{0:T(128)}, u32[]{:S(2)}) %copy-start) | copy-done | bytes 88
  0.7 28.1 %shard_map.28 = f32[2,2,48,128]{3,2,1,0:T(8,128)S(1)} custom-call(bf16[2,48,128,128]{3,2,1,0:T(8,128)(2,1)} %desc_far.1, s32[16]{0:T(128)S(1)} %copy-done), custom_call_target="tpu_custom_call" | custom-call | flops 1610612736 | bytes 4194304 | tf_op jit(solution)/shard_map/pallas_call | solution.py:354
  28.7 0.6 %copy.4 = f32[2,2,48,128]{3,2,1,0:T(8,128)} copy(f32[2,2,48,128]{3,2,1,0:T(8,128)S(1)} %shard_map.28) | data formatting | bytes 196608
Async XLA Ops:
  0.0 0.7 %copy-start = (s32[16]{0:T(128)S(1)}, s32[16]{0:T(128)}, u32[]{:S(2)}) copy-start(s32[16]{0:T(128)} %steps_far.1) | copy-start | bytes 196

commit v3 on v2

--- a/solution.py
+++ b/solution.py
@@ -155,11 +155,19 @@
             device_id=target, device_id_type=pl.DeviceIdType.MESH,
         )
 
-    def main_copy(k):
-        part = pl.ds(pl.multiple_of(k * POOL, POOL), POOL)
+    def rows_copy(first, size, k):
+        part = pl.ds(first, size)
         return remote(
             sending.at[part], incoming.at[part], main_send.at[k], main_recv.at[k], {"sec": i - 1}
         )
+
+    def main_copy(k):
+        return rows_copy(pl.multiple_of(k * POOL, POOL), POOL, k)
+
+    split = chunks - 2
+
+    def half_copy(half):
+        return rows_copy(split * POOL + half * (POOL // 2), POOL // 2, split if half == 0 else chunks)
 
     def gather_copy(d):
         slot = coarse.at[:, t]
@@ -223,21 +231,17 @@
 
     def fill(k):
         for r in range(POOL):
-            sending[k * POOL + r] = desc[chosen, k * POOL + r]
+            at = k * POOL + r
+            sending[at] = jnp.where(chosen == 0, desc[0, at], desc[1, at])
 
     load(0).wait()
+    fill(0)
+    pl.semaphore_wait(barrier, tiles - 1 + jnp.where(gives, 1, 0) + jnp.where(takes, 1, 0))
+    pl.when(gives)(lambda: main_copy(0).start())
     load(chunks - 1).wait()
+    fill(chunks - 1)
+    pl.when(gives)(lambda: main_copy(chunks - 1).start())
     loop(1, chunks - 1, lambda k: load(k).wait())
-    fill(0)
-    fill(chunks - 1)
-    pl.semaphore_wait(barrier, tiles - 1 + jnp.where(gives, 1, 0) + jnp.where(takes, 1, 0))
-
-    @pl.when(gives)
-    def _():
-        main_copy(0).start()
-        main_copy(chunks - 1).start()
-
-    start_edges(near_source, near_edge, near_sems)
 
     def pool(k):
         means = []
@@ -258,11 +262,20 @@
     def _():
         hop_copy().start()
 
+    start_edges(near_source, near_edge, near_sems)
+
     def pass_on(k):
         fill(k)
         pl.when(gives)(lambda: main_copy(k).start())
 
-    loop(1, chunks - 1, pass_on)
+    loop(1, split, pass_on)
+    fill(split)
+
+    @pl.when(gives)
+    def _():
+        half_copy(0).start()
+        half_copy(1).start()
+
     total = tiles * chunks
     loop(0, rows, lambda r: widen_row(wide, r + WIN, desc[1, r]))
     for d in range(1, tiles):
@@ -294,6 +307,13 @@
         0, chunks,
         lambda g: flow_group(wide, lambda top, col: desc[0, pl.ds(top, 8), col : col + 16, :], prior, near, g),
     )
+
+    def write(g):
+        part = pl.ds(pl.multiple_of(g * POOL, POOL), POOL)
+        for c in range(2):
+            first = jnp.where(own_first == 1, near[c, g], jnp.where(own_first == 2, far[c, g], 0.0))
+            out[0, c, part] = block_transpose(first)
+            out[1, c, part] = block_transpose(jnp.where(own_second > 0, far[c, g], 0.0))
 
     @pl.when(takes)
     def _():
@@ -307,15 +327,24 @@
         fill_prior(prior, shift_row, shift_col)
         receive_edges(incoming, far_edge, far_sems)
 
+        def widen_half(half):
+            half_copy(half).wait_recv()
+            first = split * POOL + half * (POOL // 2)
+            for r in range(POOL // 2):
+                widen_row(wide, first + r + WIN, incoming[first + r])
+
         def group(g):
-            @pl.when(g < chunks - 2)
+            @pl.when(g + 1 < split)
             def _():
                 main_copy(g + 1).wait_recv()
                 first = (g + 1) * POOL
                 for r in range(POOL):
                     widen_row(wide, first + r + WIN, incoming[first + r])
 
+            pl.when(g + 1 == split)(lambda: widen_half(0))
+            pl.when(g == split)(lambda: widen_half(1))
             flow_group(wide, lambda top, col: desc[sender, pl.ds(top, 8), col : col + 16, :], prior, far, g)
+            write(g)
 
         loop(0, chunks, group)
         for d in range(1, tiles):
@@ -325,15 +354,8 @@
     @pl.when(i == secs - 1)
     def _():
         far[...] = jnp.zeros(far.shape, far.dtype)
-
-    def write(g):
-        part = pl.ds(pl.multiple_of(g * POOL, POOL), POOL)
-        for c in range(2):
-            first = jnp.where(own_first == 1, near[c, g], jnp.where(own_first == 2, far[c, g], 0.0))
-            out[0, c, part] = block_transpose(first)
-            out[1, c, part] = block_transpose(jnp.where(own_second > 0, far[c, g], 0.0))
-
-    loop(0, chunks, write)
+        loop(0, chunks, write)
+
     for d in range(1, tiles):
         gather_copy(d).wait_send()
     finish_edges(near_source, near_edge, near_sems)
@@ -341,7 +363,10 @@
     @pl.when(gives)
     def _():
         hop_copy().wait_send()
-        loop(0, chunks, lambda k: main_copy(k).wait_send())
+        loop(0, split, lambda k: main_copy(k).wait_send())
+        main_copy(chunks - 1).wait_send()
+        half_copy(0).wait_send()
+        half_copy(1).wait_send()
 
 
 def body(descriptors, partner_step):
@@ -372,7 +397,7 @@
             pltpu.VMEM((256, 128), jnp.float32),
             pltpu.VMEM(result, jnp.float32),
             pltpu.VMEM(result, jnp.float32),
-            dma((chunks,)), dma((chunks,)), dma((2,)), dma((2,)), dma((2,)), dma((2,)),
+            dma((chunks + 1,)), dma((chunks + 1,)), dma((2,)), dma((2,)), dma((2,)), dma((2,)),
             dma((tiles,)), dma((tiles,)), dma, dma, dma((tiles,)), dma((tiles,)),
         ],
         compiler_params=pltpu.CompilerParams(
@@ -381,7 +406,7 @@
         cost_estimate=pl.CostEstimate(
             flops=4 * 256 * 256 * rows * cols, bytes_accessed=2**22, transcendentals=512 * rows * cols
         ),
-    )(descriptors, partner_step)
+    )(descriptors, pltpu.with_memory_space_constraint(partner_step, pltpu.HBM))
 
 
 def solution(mesh):

time: 29.5 us -> 27.4 us (0.929)
  Pallas kernels: 28.1 us -> 26.6 us
  local copies, waits for them, and re-layouts: 1.3 us -> 0.64 us
    pallas_call x1, Pallas kernels: 28.1 us -> 26.6 us  [body(): pl.pallas_call(functools.partial(kernel, secs, tiles), out_shape=jax.Shap...]
    unnamed x3 -> x1, local copies, waits for them, and re-layouts: 1.3 us -> 0.64 us
where the time goes in v3:
time: 27.4 us; the launch traced here: 27.2 us
  Pallas kernels  26.6 us (97%)
  local copies, waits for them, and re-layouts  0.64 us (2%)
    pallas_call x1, Pallas kernels, body(): pl.pallas_call(functools.partial(kernel, secs, tiles), out_shape=jax.Shap...  26.6 us
    unnamed x1, local copies, waits for them, and re-layouts  0.64 us

profile of v3, /device:TPU:1, one launch (start us, length us, event | category | flops | bytes accessed | tf_op | source)
XLA Modules:
  0.0 27.2 jit_solution(11575614071401802377)
XLA Ops:
  0.0 26.6 %shard_map.28 = f32[2,2,48,128]{3,2,1,0:T(8,128)S(1)} custom-call(bf16[2,48,128,128]{3,2,1,0:T(8,128)(2,1)} %desc_far.1, s32[16]{0:T(128)} %steps_far.1), custom_call_target="tpu_custom_call" | custom-call | flops 1610612736 | bytes 4194304 | tf_op jit(solution)/shard_map/pallas_call | solution.py:379
  26.6 0.6 %copy.4 = f32[2,2,48,128]{3,2,1,0:T(8,128)} copy(f32[2,2,48,128]{3,2,1,0:T(8,128)S(1)} %shard_map.28) | data formatting | bytes 196608

commit v4 on v3

--- a/solution.py
+++ b/solution.py
@@ -136,6 +136,19 @@
     i, t = lax.axis_index("sec"), lax.axis_index("tile")
     gives, takes = i > 0, i < secs - 1
 
+    def peer(d):
+        return lax.rem(t + d, tiles)
+
+    barrier = pltpu.get_barrier_semaphore()
+
+    def greet(target):
+        pl.semaphore_signal(barrier, inc=1, device_id=target, device_id_type=pl.DeviceIdType.MESH)
+
+    pl.when(gives)(lambda: greet({"sec": i - 1}))
+    pl.when(takes)(lambda: greet({"sec": i + 1}))
+    for d in range(1, tiles):
+        greet({"tile": peer(d)})
+
     def load(k):
         part = pl.ds(pl.multiple_of(k * POOL, POOL), POOL)
         return pltpu.make_async_copy(desc_far.at[:, part], desc.at[:, part], load_sem.at[k])
@@ -146,9 +159,6 @@
     load(chunks - 1).start()
     loop(1, chunks - 1, lambda k: load(k).start())
 
-    def peer(d):
-        return lax.rem(t + d, tiles)
-
     def remote(src, dst, send, recv, target):
         return pltpu.make_async_remote_copy(
             src_ref=src, dst_ref=dst, send_sem=send, recv_sem=recv,
@@ -212,16 +222,6 @@
         for r in range(WIN):
             widen_row(wide, r, edge[0, r])
             widen_row(wide, rows + WIN + r, edge[1, r])
-
-    barrier = pltpu.get_barrier_semaphore()
-
-    def greet(target):
-        pl.semaphore_signal(barrier, inc=1, device_id=target, device_id_type=pl.DeviceIdType.MESH)
-
-    for d in range(1, tiles):
-        greet({"tile": peer(d)})
-    pl.when(gives)(lambda: greet({"sec": i - 1}))
-    pl.when(takes)(lambda: greet({"sec": i + 1}))
 
     padded[...] = jnp.zeros(padded.shape, padded.dtype)
     steps_load.wait()

time: 27.4 us -> 27.4 us (level)
  no operation moved by 1% of the time
where the time goes in v4:
time: 27.4 us; the launch traced here: 27.2 us
  Pallas kernels  26.6 us (97%)
  local copies, waits for them, and re-layouts  0.64 us (2%)
    pallas_call x1, Pallas kernels, body(): pl.pallas_call(functools.partial(kernel, secs, tiles), out_shape=jax.Shap...  26.6 us
    unnamed x1, local copies, waits for them, and re-layouts  0.64 us

profile of v4, /device:TPU:1, one launch (start us, length us, event | category | flops | bytes accessed | tf_op | source)
XLA Modules:
  0.0 27.2 jit_solution(16439427717942324169)
XLA Ops:
  0.0 26.6 %shard_map.28 = f32[2,2,48,128]{3,2,1,0:T(8,128)S(1)} custom-call(bf16[2,48,128,128]{3,2,1,0:T(8,128)(2,1)} %desc_far.1, s32[16]{0:T(128)} %steps_far.1), custom_call_target="tpu_custom_call" | custom-call | flops 1610612736 | bytes 4194304 | tf_op jit(solution)/shard_map/pallas_call | solution.py:379
  26.6 0.6 %copy.4 = f32[2,2,48,128]{3,2,1,0:T(8,128)} copy(f32[2,2,48,128]{3,2,1,0:T(8,128)S(1)} %shard_map.28) | data formatting | bytes 196608
